TPU v7x, 32 devices: a whole 2x2x4 slice. The times are simulated.
32 devices in a mesh: seq: 8 (over z, y), head: 4 (over x, core).
Axes of the slice: x: 2, y: 2, z: 4, core: 2. Of those that a mesh axis runs over, the one named last changes fastest.
Arguments:
- mamba_inner: bfloat16 [1024, 3072], P('seq', 'head'), may hold values from -6 to 6
- mamba_groups: bfloat16 [1024, 512], P('seq'), may hold values from -6 to 6
- selective_gate: bfloat16 [1024, 3072], P('seq', 'head'), may hold values from -6 to 6
- step_raw: float32 [48, 1024], P('head', 'seq'), may hold values from -3 to 3
- step_bias: float32 [48], P('head'), may hold values from -0.5 to 0.5
- decay_log: float32 [48], P('head'), may hold values from -12 to -2
- conv_inner: float32 [4, 3072], P(None, 'head'), may hold values from -3 to 3
- conv_groups: float32 [4, 512], replicated, may hold values from -3 to 3
- gated_norm_gain: float32 [3072], P('head'), may hold values from 0.1 to 1.9
- query_rows: bfloat16 [1024, 1024], P('seq', 'head'), may hold values from -8 to 8
- key_rows: bfloat16 [1024, 256], P('seq'), may hold values from -8 to 8
- value_rows: bfloat16 [1024, 256], P('seq'), may hold values from -6 to 6
- segment_ids: int32 [1024], P('seq'), may hold values from 0 to 15, never falling along the last dimension, each value on 1 to 682 neighbouring positions
- mamba_proj: bfloat16 [3072, 2048], P('head'), may hold values from -0.109375 to 0.109375
- attn_proj: bfloat16 [1024, 2048], P('head'), may hold values from -0.1875 to 0.1875
Outputs:
- mixed: bfloat16 [1024, 2048], P('seq', 'head')
Inputs may be any that keep to these rules, and one draw needn't show every extreme that they name: `segment_ids`: prompt numbers never fall along the tokens; each prompt holds 1 to 682 tokens and one holds exactly 682.
All inputs are finite; a program needn't handle non-finite values.
Results may differ from a plain program's by a relative error of at most 0.015.
Values may be sent and summed in bfloat16 or wider, within the bound.
A program may use at most 128 MiB of HBM per device.

v0:
```python
import functools
import math

import jax
import jax.numpy as jnp
from jax import lax
from jax.experimental import pallas as pl
from jax.experimental.pallas import tpu as pltpu
from jax.sharding import PartitionSpec as P

HEAD_CHANNELS = 64
STATE_SIZE = 256
QH = 8
KVH = 2
HD = 128
LANES = 128
RIM = 16
F32 = jnp.float32
BF16 = jnp.bfloat16
MESH = pl.DeviceIdType.MESH
HIGHEST = lax.Precision.HIGHEST


def dot(a, b, contract, precision=None):
    return lax.dot_general(
        a, b, ((contract[:1], contract[1:]), ((), ())), precision=precision, preferred_element_type=F32
    )


def iota(shape, axis):
    return lax.broadcasted_iota(jnp.int32, shape, axis)


def column(row):
    n = row.shape[1]
    eye = iota((n, n), 0) == iota((n, n), 1)
    return jnp.sum(jnp.where(eye, jnp.broadcast_to(row, (n, n)), 0.0), axis=1, keepdims=True)


def kernel(
    n_seq,
    n_head,
    inner_hbm,
    groups_hbm,
    gate_hbm,
    step_hbm,
    bias_hbm,
    decay_hbm,
    taps_inner_hbm,
    taps_groups_hbm,
    gain_hbm,
    query_hbm,
    key_hbm,
    value_hbm,
    segs_hbm,
    mamba_proj_hbm,
    attn_proj_hbm,
    out_ref,
    inner_ref,
    groups_ref,
    gate_ref,
    step_ref,
    bias_ref,
    decay_ref,
    taps_inner_ref,
    taps_groups_ref,
    gain_ref,
    query_ref,
    key_ref,
    value_ref,
    segs_ref,
    mproj,
    aproj,
    pad_inner,
    pad_groups,
    rim_inner,
    rim_groups,
    meta,
    kv,
    conv_x,
    conv_bc,
    cumx,
    y_ref,
    state,
    s_send,
    s_recv,
    e_send,
    e_recv,
    f_send,
    f_recv,
    partner_c,
    entering,
    through,
    both,
    rs_send,
    rs_recv,
    load_sem,
    weight_sem,
    rim_sem,
    meta_ss,
    meta_rs,
    kv_ss,
    kv_rs,
    share_ss,
    share_rs,
    c_ss,
    c_rs,
    s_ss,
    s_rs,
    e_ss,
    e_rs,
    f_ss,
    f_rs,
    rs_ss,
    rs_rs,
):
    tokens, channels = inner_ref.shape
    heads = step_ref.shape[0]
    half = channels // 2
    chunks = half // LANES
    pairs = channels // LANES
    me = lax.axis_index("seq")
    mine = lax.axis_index("head")
    pair, side = me // 2, me % 2
    last_pair = n_seq // 2 - 1
    heads_here = query_ref.shape[1] // HD
    core = mine % 2
    sibling = mine + 1 - 2 * core
    opposite = (mine + 2) % n_head
    opposite_sibling = (sibling + 2) % n_head

    def at_seq(s):
        return (s, mine)

    def at_head(h):
        return (me, h)

    weights = [
        pltpu.make_async_copy(mamba_proj_hbm, mproj, weight_sem.at[0]),
        pltpu.make_async_copy(attn_proj_hbm, aproj, weight_sem.at[1]),
    ]
    loads = [
        pltpu.make_async_copy(src, dst, load_sem.at[i])
        for i, (src, dst) in enumerate(
            (
                (step_hbm, step_ref),
                (bias_hbm, bias_ref),
                (decay_hbm, decay_ref),
                (segs_hbm, segs_ref),
                (key_hbm, key_ref),
                (value_hbm, value_ref),
                (inner_hbm, inner_ref),
                (groups_hbm, groups_ref),
                (taps_inner_hbm, taps_inner_ref),
                (taps_groups_hbm, taps_groups_ref),
                (query_hbm, query_ref),
                (gate_hbm, gate_ref),
                (gain_hbm, gain_ref),
            )
        )
    ]
    for w in loads + weights:
        w.start()

    barrier = pltpu.get_barrier_semaphore()
    for d in range(1, n_seq):
        pl.semaphore_signal(barrier, inc=1, device_id=at_seq((me + d) % n_seq), device_id_type=MESH)
    for d in range(1, n_head):
        pl.semaphore_signal(barrier, inc=1, device_id=at_head((mine + d) % n_head), device_id_type=MESH)

    for w in loads[:6]:
        w.wait()
    kv_head = mine * heads_here // (QH // KVH)
    kv_cols = pl.ds(pl.multiple_of(kv_head * HD, HD), HD)
    kv[me, 0] = key_ref[:, kv_cols]
    kv[me, 1] = value_ref[:, kv_cols]

    raw = step_ref[...] + column(bias_ref[...].reshape(1, heads))
    steps = jnp.maximum(raw, 0.0) + jnp.log1p(jnp.exp(-jnp.abs(raw)))
    rates = jnp.exp(column(decay_ref[...].reshape(1, heads)))
    row_t, col_t = iota((tokens, tokens), 0), iota((tokens, tokens), 1)
    upto = (row_t <= col_t).astype(F32)
    cumul = dot(-steps * rates, upto, (1, 0), HIGHEST)
    spread = (iota((heads, channels), 1) // HEAD_CHANNELS == iota((heads, channels), 0)).astype(F32)
    cumx[...] = dot(cumul, spread, (0, 0), HIGHEST)
    stepx = dot(steps, spread, (0, 0), HIGHEST)
    total_row = cumx[tokens - 1 : tokens, :]
    segs_row = segs_ref[...].reshape(1, tokens).astype(F32)
    segs_col = column(segs_row)
    last_seg = segs_row[:, tokens - 1 : tokens]
    eye = (iota((heads, heads), 0) == iota((heads, heads), 1)).astype(F32)
    cum_cols = dot(cumul, eye, (0, 0), HIGHEST)
    meta[me] = jnp.zeros(meta.shape[1:], F32)
    meta[me, 0:1, 0:heads] = cum_cols[tokens - 1 : tokens, :]
    meta[me, 1:2, :] = segs_row
    meta[me, 2:3, :] = jnp.broadcast_to(last_seg, (1, tokens))
    for w in loads[6:]:
        w.wait()
    pl.semaphore_wait(barrier, n_seq + n_head - 2)

    def rim_copies(target):
        tail = pl.ds(tokens - RIM, RIM)
        return [
            pltpu.make_async_remote_copy(
                src.at[tail, :], dst, rim_sem.at[0, i], rim_sem.at[1, i], device_id=at_seq(target), device_id_type=MESH
            )
            for i, (src, dst) in enumerate(((inner_ref, rim_inner), (groups_ref, rim_groups)))
        ]

    def meta_copy(slot, other):
        return pltpu.make_async_remote_copy(
            meta.at[slot], meta.at[slot], meta_ss.at[other], meta_rs.at[slot], device_id=at_seq(other), device_id_type=MESH
        )

    def kv_copy(slot, other):
        return pltpu.make_async_remote_copy(
            kv.at[slot, core],
            kv.at[slot, core],
            kv_ss.at[other],
            kv_rs.at[slot],
            device_id=at_seq(other),
            device_id_type=MESH,
        )

    def kv_share(slot):
        return pltpu.make_async_remote_copy(
            kv.at[slot, core],
            kv.at[slot, core],
            share_ss.at[slot],
            share_rs.at[slot],
            device_id=at_head(sibling),
            device_id_type=MESH,
        )

    following = lax.min(me + 1, n_seq - 1)
    previous = lax.max(me - 1, 0)

    @pl.when(me < n_seq - 1)
    def _():
        for c in rim_copies(following):
            c.start()

    def send_meta(d, _):
        meta_copy(me, (me + d) % n_seq).start()
        return 0

    lax.fori_loop(1, n_seq, send_meta, 0)

    def send_kv(k, _):
        kv_copy(me, k).start()
        return 0

    lax.fori_loop(me + 1, n_seq, send_kv, 0)

    pad_inner[RIM:, :] = inner_ref[...].astype(F32)
    pad_groups[RIM:, :] = groups_ref[...].astype(F32)

    @pl.when(me > 0)
    def _():
        meta_copy(previous, previous).wait_recv()
        for c in rim_copies(previous):
            c.wait_recv()

    @pl.when(me == 0)
    def _():
        rim_inner[...] = jnp.zeros_like(rim_inner)
        rim_groups[...] = jnp.zeros_like(rim_groups)

    pad_inner[0:RIM, :] = rim_inner[...].astype(F32)
    pad_groups[0:RIM, :] = rim_groups[...].astype(F32)

    taps = taps_inner_ref.shape[0]
    prev_last = meta[previous, 2:3, 0:1]
    prev_segs = meta[previous, 1:2, :]
    token_col = iota((tokens, 1), 0)
    keeps = []
    for k in range(taps - 1):
        back = taps - 1 - k
        own = jnp.sum(
            jnp.where(row_t - back == col_t, jnp.broadcast_to(segs_row, (tokens, tokens)), 0.0), 1, keepdims=True
        )
        before = jnp.sum(
            jnp.where(row_t - back + tokens == col_t, jnp.broadcast_to(prev_segs, (tokens, tokens)), 0.0),
            1,
            keepdims=True,
        )
        keeps.append(jnp.where(token_col >= back, own, before) == segs_col)

    def conv(pad, weight_ref, out):
        for c in range(0, out.shape[1], LANES):
            cols = slice(c, c + LANES)
            acc = jnp.zeros((tokens, LANES), F32)
            for k in range(taps):
                first = RIM - (taps - 1) + k
                term = weight_ref[k : k + 1, cols] * pad[first : first + tokens, cols]
                acc = acc + (jnp.where(keeps[k], term, 0.0) if k < taps - 1 else term)
            out[:, cols] = jax.nn.silu(acc).astype(BF16)

    conv(pad_groups, taps_groups_ref, conv_bc)
    conv(pad_inner, taps_inner_ref, conv_x)

    read_b = conv_bc[:, :STATE_SIZE]
    read_c = conv_bc[:, STATE_SIZE:]
    in_last = segs_col == last_seg
    tail = jnp.where(in_last, jnp.exp(total_row - cumx[...]), 0.0)
    weighted = (tail * stepx * conv_x[...].astype(F32)).astype(BF16)
    state[...] = dot(read_b, weighted, (0, 0))

    partner = me + 1 - 2 * side
    upper = lax.min(me + 2, n_seq - 1)
    lower = lax.max(me - 2, 0)

    def part(which, c):
        return pl.ds(pl.multiple_of(which * half + c * LANES, LANES), LANES)

    def hop(src, dst, ss, rs, c, target):
        return pltpu.make_async_remote_copy(
            src.at[c], dst.at[c], ss.at[c], rs.at[c], device_id=at_seq(target), device_id_type=MESH
        )

    depth = STATE_SIZE // 2
    for i in range(2 * chunks):
        c, r = i // 2, i % 2
        s_send[i] = state[r * depth : (r + 1) * depth, part(1 - side, c)].astype(BF16)
        hop(s_send, s_recv, s_ss, s_rs, i, partner).start()

    def c_copy():
        return pltpu.make_async_remote_copy(
            conv_bc.at[:, pl.ds(STATE_SIZE, STATE_SIZE)],
            partner_c,
            c_ss.at[0],
            c_rs.at[0],
            device_id=at_seq(partner),
            device_id_type=MESH,
        )

    c_copy().start()

    def wait_meta(d, _):
        k = (me + d) % n_seq
        meta_copy(k, k).wait_recv()
        return 0

    lax.fori_loop(1, n_seq - 1, wait_meta, 0)

    @pl.when(me == 0)
    def _():
        meta_copy(n_seq - 1, n_seq - 1).wait_recv()

    crossing = dot(read_c, read_b, (1, 1))
    live = (jnp.broadcast_to(segs_row, (tokens, tokens)) == segs_col) & (row_t >= col_t)
    left = iota((tokens, LANES), 1) < HEAD_CHANNELS
    for p in range(pairs):
        got = []
        for h in (2 * p, 2 * p + 1):
            decays = jnp.exp(jnp.where(live, cum_cols[:, h : h + 1] - cumul[h : h + 1, :], -jnp.inf))
            mixing = (crossing * decays * steps[h : h + 1, :]).astype(BF16)
            got.append(dot(mixing, conv_x[:, p * LANES : (p + 1) * LANES], (1, 0)))
        y_ref[:, p * LANES : (p + 1) * LANES] = jnp.where(left, got[0], got[1])

    scale = 1.0 / math.sqrt(HD)
    queries = jnp.concatenate([query_ref[:, h * HD : (h + 1) * HD] for h in range(heads_here)], axis=0)
    rows = heads_here * tokens
    segs_rows = jnp.concatenate([segs_col] * heads_here, axis=0)
    token_rows = jnp.concatenate([token_col] * heads_here, axis=0)

    def share(d, _):
        kv_copy(me - d, me).wait_recv()
        kv_share(me - d).start()
        return 0

    def attend(d, carry):
        top, total, summed = carry
        k = me - d

        @pl.when(d > 0)
        def _():
            kv_share(k).wait_recv()

        scores = dot(queries, kv[k, 0], (1, 1)) * scale
        allowed = (meta[k, 1:2, :] == segs_rows) & (
            iota((rows, tokens), 1) + (k - me) * tokens <= token_rows
        )
        scores = jnp.where(allowed, scores, -jnp.inf)
        new_top = jnp.maximum(top, jnp.max(scores, axis=1, keepdims=True))
        rescale = jnp.exp(top - new_top)
        w = jnp.exp(scores - new_top)
        total = total * rescale + jnp.sum(w, axis=1, keepdims=True)
        summed = summed * rescale + dot(w.astype(BF16), kv[k, 1], (1, 0))
        return new_top, total, summed

    def attention():
        lax.fori_loop(1, me + 1, share, 0)
        top, total, summed = lax.fori_loop(
            0,
            me + 1,
            attend,
            (jnp.full((rows, 1), -1e30, F32), jnp.zeros((rows, 1), F32), jnp.zeros((rows, HD), F32)),
        )
        attended = (summed / total).astype(BF16)
        for h in range(heads_here):
            both[:, channels + h * HD : channels + (h + 1) * HD] = attended[h * tokens : (h + 1) * tokens]

    pl.when(me >= n_seq // 2)(attention)

    @pl.when(pair == 0)
    def _():
        e_recv[...] = jnp.zeros_like(e_recv)

    first, second = pair * 2, pair * 2 + 1
    seg_before = meta[lax.max(first - 1, 0), 2:3, 0:1]
    seg_first = meta[first, 2:3, 0:1]
    seg_second = meta[second, 2:3, 0:1]
    through[0:1, :] = jnp.where(
        seg_first == seg_before, jnp.exp(dot(meta[first, 0:1, 0:heads], spread, (1, 0), HIGHEST)), 0.0
    )
    through[1:2, :] = jnp.where(
        seg_second == seg_first, jnp.exp(dot(meta[second, 0:1, 0:heads], spread, (1, 0), HIGHEST)), 0.0
    )
    through[2:3, :] = gain_ref[...].reshape(1, channels)
    c_copy().wait_recv()
    on_left = side == 0
    for c in range(chunks):
        cols = part(side, c)
        through_first = through[0:1, cols]
        through_second = through[1:2, cols]
        theirs = []
        for r in range(2):
            i, span = 2 * c + r, slice(r * depth, (r + 1) * depth)
            hop(s_send, s_recv, s_ss, s_rs, i, partner).wait_recv()
            own, others = state[span, cols], s_recv[i].astype(F32)

            @pl.when(pair > 0)
            def _():
                hop(e_send, e_recv, e_ss, e_rs, i, lower).wait_recv()

            enter_first = e_recv[i].astype(F32)
            enter_second = through_first * enter_first + jnp.where(on_left, own, others)

            @pl.when(pair < last_pair)
            def _():
                e_send[i] = (through_second * enter_second + jnp.where(on_left, others, own)).astype(BF16)
                hop(e_send, e_recv, e_ss, e_rs, i, upper).start()

            theirs.append(jnp.where(on_left, enter_second, enter_first).astype(BF16))
            entering[c, span, :] = jnp.where(on_left, enter_first, enter_second).astype(BF16)

        f_send[c] = dot(partner_c[...], jnp.concatenate(theirs, axis=0), (1, 0)).astype(BF16)
        hop(f_send, f_recv, f_ss, f_rs, c, partner).start()

    joined = segs_col == prev_last
    same_head = (iota((LANES, LANES), 0) // HEAD_CHANNELS == iota((LANES, LANES), 1) // HEAD_CHANNELS).astype(F32)

    def norm(cols, carried):
        y = y_ref[:, cols] + jnp.where(joined, jnp.exp(cumx[:, cols]), 0.0) * carried
        gated = y * jax.nn.silu(gate_ref[:, cols].astype(F32))
        mean_square = dot(gated * gated, same_head, (1, 0), HIGHEST) * (1.0 / HEAD_CHANNELS)
        both[:, cols] = (gated * lax.rsqrt(mean_square + 1e-05) * through[2:3, cols]).astype(BF16)

    pl.when(me < n_seq // 2)(attention)
    for c in range(chunks):
        norm(part(side, c), dot(read_c, entering[c], (1, 0)))
    for c in range(chunks):
        hop(f_send, f_recv, f_ss, f_rs, c, partner).wait_recv()
        norm(part(1 - side, c), f_recv[c].astype(F32))

    for w in weights:
        w.wait()
    width = out_ref.shape[1]

    def product(j, part_of):
        cols = pl.ds(pl.multiple_of(j * width + part_of * (width // 2), LANES), width // 2)
        return dot(both[:, :channels], mproj[:, cols], (1, 0)) + dot(both[:, channels:], aproj[:, cols], (1, 0))

    def rs_copy(i, target):
        return pltpu.make_async_remote_copy(
            rs_send.at[i], rs_recv.at[i], rs_ss.at[i], rs_rs.at[i], device_id=at_head(target), device_id_type=MESH
        )

    to_pair = [rs_copy(h, sibling) for h in range(2)]
    to_sibling = [rs_copy(2 + h, sibling) for h in range(2)]
    to_opposite = [rs_copy(4 + h, opposite) for h in range(2)]
    for h in range(2):
        rs_send[h] = product(opposite_sibling, h).astype(BF16)
        to_pair[h].start()
    for h in range(2):
        away = product(opposite, h)
        to_pair[h].wait_recv()
        rs_send[4 + h] = (away + rs_recv[h].astype(F32)).astype(BF16)
        to_opposite[h].start()
    for h in range(2):
        rs_send[2 + h] = product(sibling, h).astype(BF16)
        to_sibling[h].start()
    for h in range(2):
        result = product(mine, h)
        to_sibling[h].wait_recv()
        result = result + rs_recv[2 + h].astype(F32)
        to_opposite[h].wait_recv()
        out_ref[:, h * (width // 2) : (h + 1) * (width // 2)] = (result + rs_recv[4 + h].astype(F32)).astype(BF16)

    for copy in (*to_pair, *to_sibling, *to_opposite, c_copy()):
        copy.wait_send()

    def sent_share(d, _):
        kv_share(me - d).wait_send()
        return 0

    lax.fori_loop(1, me + 1, sent_share, 0)

    @pl.when(me < n_seq - 1)
    def _():
        for c in rim_copies(following):
            c.wait_send()

    def sent_meta(d, _):
        meta_copy(me, (me + d) % n_seq).wait_send()
        return 0

    lax.fori_loop(1, n_seq, sent_meta, 0)

    def sent_kv(k, _):
        kv_copy(me, k).wait_send()
        return 0

    lax.fori_loop(me + 1, n_seq, sent_kv, 0)
    for c in range(chunks):
        hop(f_send, f_recv, f_ss, f_rs, c, partner).wait_send()
    for i in range(2 * chunks):
        hop(s_send, s_recv, s_ss, s_rs, i, partner).wait_send()

        @pl.when(pair < last_pair)
        def _():
            hop(e_send, e_recv, e_ss, e_rs, i, upper).wait_send()


def shards(n_seq, n_head, *arrays):
    (inner, groups, gate, step, bias, decay, taps_i, taps_g, gain, query, key, value, segs, mproj, aproj) = arrays
    tokens, channels = inner.shape
    out_width = mproj.shape[1] // n_head
    chunks = channels // 2 // LANES
    hops = (chunks, STATE_SIZE, LANES)
    vmem = pl.BlockSpec(memory_space=pltpu.VMEM)
    hbm = pl.BlockSpec(memory_space=pltpu.HBM)
    dma = pltpu.SemaphoreType.DMA
    scratch = [
        *[pltpu.VMEM(a.shape, a.dtype) for a in arrays[:13]],
        pltpu.VMEM(mproj.shape, BF16),
        pltpu.VMEM(aproj.shape, BF16),
        pltpu.VMEM((tokens + RIM, channels), F32),
        pltpu.VMEM((tokens + RIM, groups.shape[1]), F32),
        pltpu.VMEM((RIM, channels), BF16),
        pltpu.VMEM((RIM, groups.shape[1]), BF16),
        pltpu.VMEM((n_seq, 8, tokens), F32),
        pltpu.VMEM((n_seq, 2, tokens, HD), BF16),
        pltpu.VMEM((tokens, channels), BF16),
        pltpu.VMEM((tokens, groups.shape[1]), BF16),
        pltpu.VMEM((tokens, channels), F32),
        pltpu.VMEM((tokens, channels), F32),
        pltpu.VMEM((STATE_SIZE, channels), F32),
        *[pltpu.VMEM((2 * chunks, STATE_SIZE // 2, LANES), BF16) for _ in range(4)],
        *[pltpu.VMEM((chunks, tokens, LANES), BF16) for _ in range(2)],
        pltpu.VMEM((tokens, STATE_SIZE), BF16),
        pltpu.VMEM(hops, BF16),
        pltpu.VMEM((8, channels), F32),
        pltpu.VMEM((tokens, channels + query.shape[1]), BF16),
        pltpu.VMEM((6, tokens, out_width // 2), BF16),
        pltpu.VMEM((6, tokens, out_width // 2), BF16),
        dma((13,)),
        dma((2,)),
        dma((2, 2)),
        dma((n_seq,)),
        dma((n_seq,)),
        dma((n_seq,)),
        dma((n_seq,)),
        dma((n_seq,)),
        dma((n_seq,)),
        dma((1,)),
        dma((1,)),
        *[dma((2 * chunks,)) for _ in range(4)],
        *[dma((chunks,)) for _ in range(2)],
        dma((6,)),
        dma((6,)),
    ]
    return pl.pallas_call(
        functools.partial(kernel, n_seq, n_head),
        out_shape=jax.ShapeDtypeStruct((tokens, out_width), BF16),
        in_specs=[hbm] * 15,
        out_specs=vmem,
        scratch_shapes=scratch,
        compiler_params=pltpu.CompilerParams(
            collective_id=0, has_side_effects=True, vmem_limit_bytes=64 * 2**20
        ),
        name="mixer",
    )(
        inner,
        groups,
        gate,
        step,
        bias,
        decay,
        taps_i,
        taps_g,
        gain,
        query,
        key,
        value,
        segs,
        mproj,
        aproj,
    )


def solution(mesh):
    placed = (
        P("seq", "head"),
        P("seq", None),
        P("seq", "head"),
        P("head", "seq"),
        P("head"),
        P("head"),
        P(None, "head"),
        P(),
        P("head"),
        P("seq", "head"),
        P("seq", None),
        P("seq", None),
        P("seq"),
        P("head", None),
        P("head", None),
    )
    return jax.shard_map(
        functools.partial(shards, mesh.shape["seq"], mesh.shape["head"]),
        mesh=mesh,
        in_specs=placed,
        out_specs=P("seq", "head"),
        check_vma=False,
    )
```

profile of v0, /device:TPU:25, one launch (start us, length us, event | category | flops | bytes accessed | tf_op | source)
XLA Modules:
  0.0 36.7 jit_solution(4367709395797226314)
XLA Ops:
  0.0 35.1 %mixer.1 = bf16[128,512]{1,0:T(8,128)(2,1)} custom-call(bf16[128,768]{1,0:T(8,128)(2,1)} %inner_hbm.1, bf16[128,512]{1,0:T(8,128)(2,1)} %groups_hbm.1, bf16[128,768]{1,0:T(8,128)(2,1)} %gate_hbm.1, f32[12,128]{1,0:T(8,128)} %step_hbm.1, f32[12]{0:T(128)} %bias_hbm.1, f32[12]{0:T(128)} %decay_hbm.1, f32[4,768]{1,0:T(4,128)} %taps_inner_hbm.1, ...), custom_call_target="tpu_custom_call" | custom-call | tf_op jit(solution)/shard_map/mixer/pallas_call | solution.py:584
  35.2 1.6 %copy.17 = bf16[128,512]{1,0:T(8,128)(2,1)} copy(bf16[128,512]{1,0:T(8,128)(2,1)} %mixer.1) | data formatting | bytes 262144
where the time goes:
time: 37.4 us; the launch traced here: 36.7 us
  Pallas kernels  35.1 us (94%)
  local copies, waits for them, and re-layouts  1.57 us (4%)
    pallas_call x1, Pallas kernels, shards(): pl.pallas_call(functools.partial(kernel, n_seq, n_head), out_shape=jax.Sh...  35.1 us
    unnamed x1, local copies, waits for them, and re-layouts  1.57 us

commit v1 on v0

v1 whole, which is shorter than its diff:
```python
import functools
import math

import jax
import jax.numpy as jnp
from jax import lax
from jax.experimental import pallas as pl
from jax.experimental.pallas import tpu as pltpu
from jax.sharding import PartitionSpec as P

HEAD_CHANNELS = 64
STATE_SIZE = 256
QH = 8
KVH = 2
HD = 128
LANES = 128
RIM = 16
PIECES = 4
F32 = jnp.float32
BF16 = jnp.bfloat16
MESH = pl.DeviceIdType.MESH


def dot(a, b, contract):
    return lax.dot_general(a, b, ((contract[:1], contract[1:]), ((), ())), preferred_element_type=F32)


def iota(shape, axis):
    return lax.broadcasted_iota(jnp.int32, shape, axis)


def column(row):
    n = row.shape[1]
    eye = iota((n, n), 0) == iota((n, n), 1)
    return jnp.sum(jnp.where(eye, jnp.broadcast_to(row, (n, n)), 0.0), axis=1, keepdims=True)


def thirds(a):
    high = a.astype(BF16).astype(F32)
    rest = a - high
    middle = rest.astype(BF16).astype(F32)
    return jnp.concatenate([high, middle, rest - middle], axis=0).astype(BF16)


def to_columns(rows):
    n = rows.shape[0]
    pick = (iota((3 * n, n), 0) % n == iota((3 * n, n), 1)).astype(BF16)
    return dot(thirds(rows), pick, (0, 0))


def kernel(
    n_seq,
    n_head,
    inner_hbm,
    groups_hbm,
    gate_hbm,
    step_hbm,
    bias_hbm,
    decay_hbm,
    taps_inner_hbm,
    taps_groups_hbm,
    gain_hbm,
    query_hbm,
    key_hbm,
    value_hbm,
    segs_hbm,
    mamba_proj_hbm,
    attn_proj_hbm,
    out_ref,
    segs_ref,
    step_in,
    bias_ref,
    decay_ref,
    taps_inner_ref,
    taps_groups_ref,
    gain_ref,
    query_ref,
    gate_ref,
    x_in,
    g_in,
    rim_x,
    rim_g,
    segt,
    kv,
    pad_x,
    pad_g,
    conv_x,
    conv_b,
    conv_c,
    y_ref,
    state,
    e_send,
    e_recv,
    f_send,
    f_recv,
    both,
    mproj,
    aproj,
    rs_send,
    rs_recv,
    top_ref,
    total_ref,
    summed_ref,
    ready,
    load_sem,
    weight_sem,
    x_ss,
    x_rs,
    g_ss,
    g_rs,
    step_sem,
    rim_ss,
    rim_rs,
    seg_ss,
    seg_rs,
    kv_ss,
    kv_rs,
    share_ss,
    share_rs,
    e_ss,
    e_rs,
    f_ss,
    f_rs,
    rs_ss,
    rs_rs,
):
    tokens, channels = gate_ref.shape
    heads = step_in.shape[1]
    half = channels // 2
    few = heads // 2
    chunks = half // LANES
    wide = groups_hbm.shape[1]
    taps = taps_inner_ref.shape[0]
    depth = STATE_SIZE // PIECES
    heads_here = query_ref.shape[1] // HD
    me = lax.axis_index("seq")
    mine = lax.axis_index("head")
    pair, side = me // 2, me % 2
    other = 1 - side
    last_pair = n_seq // 2 - 1
    partner = me + 1 - 2 * side
    upper = lax.min(me + 2, n_seq - 1)
    lower = lax.max(me - 2, 0)
    following = lax.min(me + 1, n_seq - 1)
    previous = lax.max(me - 1, 0)
    core = mine % 2
    sibling = mine + 1 - 2 * core
    opposite = (mine + 2) % n_head
    opposite_sibling = (sibling + 2) % n_head
    has_upper, has_lower = pair < last_pair, pair > 0

    def at_seq(s):
        return (s, mine)

    def at_head(h):
        return (me, h)

    def remote(src, dst, ss, rs, target):
        return pltpu.make_async_remote_copy(src, dst, ss, rs, device_id=target, device_id_type=MESH)

    def part(which, c):
        return pl.ds(pl.multiple_of(which * half + c * LANES, LANES), LANES)

    def side_half(which):
        return pl.ds(pl.multiple_of(which * half, LANES), half)

    core_cols = pl.ds(pl.multiple_of(core * STATE_SIZE, STATE_SIZE), STATE_SIZE)
    kv_head = mine * heads_here // (QH // KVH)
    kv_cols = pl.ds(pl.multiple_of(kv_head * HD, HD), HD)
    body = pl.ds(0, tokens)

    weights = [
        pltpu.make_async_copy(mamba_proj_hbm, mproj, weight_sem.at[0]),
        pltpu.make_async_copy(attn_proj_hbm, aproj, weight_sem.at[1]),
    ]
    loads = [
        pltpu.make_async_copy(src, dst, load_sem.at[i])
        for i, (src, dst) in enumerate(
            (
                (segs_hbm, segs_ref),
                (key_hbm.at[:, kv_cols], kv.at[me, 0, body]),
                (value_hbm.at[:, kv_cols], kv.at[me, 1, body]),
                (groups_hbm, g_in.at[side]),
                (taps_groups_hbm, taps_groups_ref),
                (inner_hbm.at[:, side_half(side)], x_in.at[side]),
                (taps_inner_hbm.at[:, side_half(side)], taps_inner_ref),
                (step_hbm, step_in.at[side]),
                (bias_hbm, bias_ref),
                (decay_hbm, decay_ref),
                (query_hbm, query_ref),
                (gate_hbm, gate_ref),
                (gain_hbm, gain_ref),
            )
        )
    ]

    barrier = pltpu.get_barrier_semaphore()

    def hello(target):
        pl.semaphore_signal(barrier, inc=1, device_id=target, device_id_type=MESH)

    hello(at_seq(partner))
    hello(at_head(sibling))
    hello(at_head(opposite))

    def hello_later(k, _):
        hello(at_seq(k))
        return 0

    lax.fori_loop(2 * pair + 2, n_seq, hello_later, 0)
    for w in loads:
        w.start()
    pl.semaphore_wait(barrier, 3 + 2 * pair)

    def answer(k, _):
        pl.semaphore_signal(ready.at[me], inc=1, device_id=at_seq(k), device_id_type=MESH)
        return 0

    lax.fori_loop(0, 2 * pair, answer, 0)

    tail_rows = pl.ds(tokens - RIM, RIM)

    def rim_copies(kind, target, slot, which):
        return [
            remote(
                inner_hbm.at[tail_rows, side_half(which)], rim_x.at[slot], rim_ss.at[kind, 0], rim_rs.at[slot, 0], at_seq(target)
            ),
            remote(groups_hbm.at[tail_rows, :], rim_g.at[slot], rim_ss.at[kind, 1], rim_rs.at[slot, 1], at_seq(target)),
        ]

    def rim_next():
        return rim_copies(0, following, other, other)

    def rim_skip():
        return rim_copies(1, upper, 0, side)

    def group_copy(block):
        return remote(
            groups_hbm.at[:, core_cols], g_in.at[block, :, core_cols], g_ss.at[0], g_rs.at[0], at_seq(partner)
        )

    def group_share():
        return remote(
            g_in.at[other, :, core_cols], g_in.at[other, :, core_cols], g_ss.at[1], g_rs.at[1], at_head(sibling)
        )

    def x_copy(block, c):
        return remote(
            inner_hbm.at[:, part(other, c)],
            x_in.at[block, :, pl.ds(c * LANES, LANES)],
            x_ss.at[c],
            x_rs.at[c],
            at_seq(partner),
        )

    def step_copy(block):
        return remote(step_hbm, step_in.at[block], step_sem.at[0], step_sem.at[1], at_seq(partner))

    loads[0].wait()
    own_segs = jnp.broadcast_to(segs_ref[...].reshape(1, tokens).astype(F32), (RIM, tokens)).astype(BF16)
    segt[1 + side] = own_segs

    def seg_copy(kind, target, src, dst):
        return remote(segt.at[src], segt.at[dst], seg_ss.at[kind], seg_rs.at[dst], at_seq(target))

    step_copy(side).start()
    seg_copy(0, partner, 1 + side, 1 + side).start()

    @pl.when(side == 0)
    def _():
        for c in rim_next():
            c.start()

    group_copy(side).start()
    for c in range(chunks):
        x_copy(side, c).start()

    def kv_copy(b, k):
        return remote(kv.at[b, core], kv.at[b, core], kv_ss.at[k], kv_rs.at[b], at_seq(k))

    def kv_share(b):
        return remote(kv.at[b, core], kv.at[b, core], share_ss.at[b], share_rs.at[b], at_head(sibling))

    def pass_on(d, _):
        kv_copy(me - d, partner).wait_recv()
        kv_share(me - d).start()
        return 0

    def conv_flags(b, before):
        now = segt[b + 1].astype(F32)[0:8]
        both_blocks = jnp.concatenate([before, now], axis=1)
        row = iota((8, tokens), 0)
        flags = now
        for back in range(1, taps):
            kept = (pltpu.roll(both_blocks, back, 1)[:, tokens:] == now).astype(F32)
            flags = jnp.where(row == back, kept, flags)
        eye = (iota((8, 8), 0) == iota((8, 8), 1)).astype(BF16)
        return dot(flags.astype(BF16), eye, (0, 0))

    def keeps_of(flags, n):
        return [jnp.broadcast_to(flags[:n, back : back + 1], (n, LANES)) > 0.5 for back in range(taps - 1, 0, -1)]

    def conv(pad, b, cols, keeps, weight_ref, n):
        acc = weight_ref[taps - 1 : taps, cols] * pad[b, RIM : RIM + n, cols]
        for k in range(taps - 1):
            first = RIM - (taps - 1) + k
            term = weight_ref[k : k + 1, cols] * pad[b, first : first + n, cols]
            acc = acc + jnp.where(keeps[k], term, 0.0)
        return jax.nn.silu(acc).astype(BF16)

    def conv_groups(b, keeps, n):
        for out, base in ((conv_b, 0), (conv_c, STATE_SIZE)):
            for c in range(0, STATE_SIZE, LANES):
                at = slice(base + c, base + c + LANES)
                out[b, 0:n, c : c + LANES] = conv(pad_g, b, at, keeps, taps_groups_ref, n)

    def conv_inner(b, c, keeps, n):
        at = slice(c * LANES, (c + 1) * LANES)
        conv_x[b, 0:n, at] = conv(pad_x, b, at, keeps, taps_inner_ref, n)

    def rim_arrived(slot):
        for c in rim_copies(0, partner, slot, slot):
            c.wait_recv()

    for w in loads[3:7]:
        w.wait()
    pad_g[side, 0:RIM, :] = jnp.zeros((RIM, wide), F32)
    pad_x[side, 0:RIM, :] = jnp.zeros((RIM, half), F32)
    pad_g[side, RIM:, :] = g_in[side].astype(F32)
    pad_x[side, RIM:, :] = x_in[side].astype(F32)
    own_flags = conv_flags(side, jnp.full((8, tokens), -1.0, F32))
    own_keeps = keeps_of(own_flags, tokens)
    conv_groups(side, own_keeps, tokens)

    kv[me, 0, pl.ds(tokens, RIM), :] = own_segs
    kv[me, 1, pl.ds(tokens, RIM), :] = own_segs
    loads[1].wait()
    loads[2].wait()

    @pl.when(side == 0)
    def _():
        kv_copy(me, partner).start()

    @pl.when(has_upper)
    def _():
        pl.semaphore_wait(ready.at[upper], 1)

    @pl.when(has_upper & (side == 1))
    def _():
        pl.semaphore_wait(ready.at[following], 1)
        seg_copy(1, following, 2, 0).start()
        seg_copy(2, upper, 2, 0).start()
        for c in rim_skip():
            c.start()
        for c in rim_next():
            c.start()
        kv_copy(me, following).start()

    @pl.when(has_upper)
    def _():
        kv_copy(me, upper).start()

    for c in range(chunks):
        conv_inner(side, c, own_keeps, tokens)

    for w in loads[7:10]:
        w.wait()
    step_copy(other).wait_recv()
    seg_copy(0, partner, 1 + other, 1 + other).wait_recv()
    bias = column(bias_ref[...].reshape(1, heads))
    rates = jnp.exp(column(decay_ref[...].reshape(1, heads)))
    on_left = side == 0

    def mine_of(a):
        kept = jnp.where(on_left, a[:few], a[few:])
        return jnp.concatenate([kept, jnp.zeros((8 - few, a.shape[1]), F32)], axis=0)

    raw = mine_of(jnp.concatenate([step_in[0], step_in[1]], axis=1) + bias)
    steps = jnp.maximum(raw, 0.0) + jnp.log1p(jnp.exp(-jnp.abs(raw)))
    span = 2 * tokens
    row_t, col_t = iota((span, span), 0), iota((span, span), 1)
    upto = (row_t <= col_t).astype(BF16)
    sums = dot(thirds(-steps * mine_of(rates)), upto, (1, 0))
    cumul = sums[0:8] + sums[8:16] + sums[16:24]
    total = cumul[:, span - 1 : span]
    segs_rows8 = jnp.concatenate([segt[1].astype(F32)[0:8], segt[2].astype(F32)[0:8]], axis=1)
    last_seg = segs_rows8[:, span - 1 : span]
    weigh = jnp.where(segs_rows8 == last_seg, jnp.exp(total - cumul), 0.0) * steps
    cols = to_columns(jnp.concatenate([cumul, weigh, jnp.exp(cumul), segs_rows8], axis=0))
    left = iota((span, LANES), 1) < HEAD_CHANNELS

    def two_heads(base, c):
        a, b = base + 2 * c, base + 2 * c + 1
        return jnp.where(left, cols[:, a : a + 1], cols[:, b : b + 1])

    group_copy(other).wait_recv()
    group_share().start()

    @pl.when(has_lower)
    def _():
        seg_copy(0, partner, 0, 0).wait_recv()
        rim_arrived(0)

    @pl.when(pair == 0)
    def _():
        segt[0] = jnp.full((RIM, tokens), -1.0, BF16)
        rim_x[0] = jnp.zeros_like(rim_x[0])
        rim_g[0] = jnp.zeros_like(rim_g[0])

    @pl.when(side == 1)
    def _():
        rim_arrived(1)

    @pl.when(side == 0)
    def _():
        rim_x[1] = x_in[0, tokens - RIM :, :]
        rim_g[1] = g_in[0, tokens - RIM :, :]

    for b in range(2):
        pad_g[b, 0:RIM, :] = rim_g[b].astype(F32)
        pad_x[b, 0:RIM, :] = rim_x[b].astype(F32)
    first_keeps = keeps_of(conv_flags(side, segt[side].astype(F32)[0:8]), RIM)
    conv_groups(side, first_keeps, RIM)
    for c in range(chunks):
        conv_inner(side, c, first_keeps, RIM)
    prev_last = segt[0].astype(F32)[0:8, tokens - 1 : tokens]
    spread = iota((8, half), 1) // HEAD_CHANNELS == iota((8, half), 0)
    crossing_pair = jnp.where(last_seg == prev_last, jnp.exp(total), 0.0)
    through = jnp.sum(jnp.where(spread, crossing_pair, 0.0), axis=0, keepdims=True)
    joined = cols[:, 24:25] == prev_last[0:1]

    def send_far(k, _):
        pl.semaphore_wait(ready.at[k], 1)
        kv_copy(me, k).start()
        return 0

    lax.fori_loop(me + 3, n_seq, send_far, 0)

    other_keeps = keeps_of(conv_flags(other, segt[other].astype(F32)[0:8]), tokens)
    group_share().wait_recv()
    pad_g[other, RIM:, :] = g_in[other].astype(F32)
    conv_groups(other, other_keeps, tokens)
    read_b = conv_b[...].reshape(span, STATE_SIZE)
    read_c = conv_c[...].reshape(span, STATE_SIZE)

    def hop(src, dst, ss, rs, c, target):
        return remote(src.at[c], dst.at[c], ss.at[c], rs.at[c], at_seq(target))

    def e_hop(i, target):
        return hop(e_send, e_recv, e_ss, e_rs, i, target)

    for c in range(chunks):
        x_copy(other, c).wait_recv()
        lanes = slice(c * LANES, (c + 1) * LANES)
        pad_x[other, RIM:, lanes] = x_in[other, :, lanes].astype(F32)
        conv_inner(other, c, other_keeps, tokens)
        x = conv_x[:, :, lanes].reshape(span, LANES).astype(F32)
        state[:, lanes] = dot(read_b, (two_heads(8, c) * x).astype(BF16), (0, 0))

        @pl.when(pair == 0)
        def _():
            for r in range(PIECES):
                i = PIECES * c + r
                e_send[i] = state[r * depth : (r + 1) * depth, lanes].astype(BF16)
                e_hop(i, upper).start()

    for w in weights:
        w.start()

    for w in loads[10:]:
        w.wait()
    scale = 1.0 / math.sqrt(HD)
    queries = jnp.concatenate([query_ref[:, h * HD : (h + 1) * HD] for h in range(heads_here)], axis=0)
    rows = heads_here * tokens
    segs_q = jnp.concatenate([own_flags[:, 0:1]] * heads_here, axis=0)
    token_q = jnp.concatenate([iota((tokens, 1), 0)] * heads_here, axis=0)
    top_ref[...] = jnp.full((rows, 1), -1e30, F32)
    total_ref[...] = jnp.zeros((rows, 1), F32)
    summed_ref[...] = jnp.zeros((rows, HD), F32)

    def attend(d, _):
        k = me - d

        @pl.when(d > 0)
        def _():
            kv_share(k).wait_recv()

        scores = dot(queries, kv[k, 0, 0:tokens, :], (1, 1)) * scale
        segs_k = kv[k, 0, tokens:, :].astype(F32)[0:1, :tokens]
        allowed = (segs_k == segs_q) & (iota((rows, tokens), 1) + (k - me) * tokens <= token_q)
        scores = jnp.where(allowed, scores, -jnp.inf)
        top = top_ref[...]
        new_top = jnp.maximum(top, jnp.max(scores, axis=1, keepdims=True))
        rescale = jnp.exp(top - new_top)
        w = jnp.exp(scores - new_top)
        top_ref[...] = new_top
        total_ref[...] = total_ref[...] * rescale + jnp.sum(w, axis=1, keepdims=True)
        summed_ref[...] = summed_ref[...] * rescale + dot(w.astype(BF16), kv[k, 1, 0:tokens, :], (1, 0))
        return 0

    same_head = (iota((2 * LANES, LANES), 0) % LANES // HEAD_CHANNELS == iota((2 * LANES, LANES), 1) // HEAD_CHANNELS).astype(
        BF16
    )
    gain_row = gain_ref[...].reshape(1, channels)
    gains = [
        jnp.where(on_left, gain_row[:, :half], gain_row[:, half:]),
        jnp.where(on_left, gain_row[:, half:], gain_row[:, :half]),
    ]

    def norm(which, c, gain, y):
        at = part(which, c)
        gated = y * jax.nn.silu(gate_ref[:, at].astype(F32))
        square = gated * gated
        high = square.astype(BF16)
        parts = jnp.concatenate([high, (square - high.astype(F32)).astype(BF16)], axis=1)
        mean_square = dot(parts, same_head, (1, 0)) * (1.0 / HEAD_CHANNELS)
        normed = gated * lax.rsqrt(mean_square + 1e-05) * gain[:, c * LANES : (c + 1) * LANES]
        both[:, at] = normed.astype(BF16)

    def f_hop(c):
        return hop(f_send, f_recv, f_ss, f_rs, c, partner)

    @pl.when(pair == 0)
    def _():
        e_recv[...] = jnp.zeros_like(e_recv)

    live = (cols[:, 24:25] == segs_rows8[0:1]) & (row_t >= col_t)
    crossing = dot(read_c, read_b, (1, 1))
    for c in range(chunks):
        lanes = slice(c * LANES, (c + 1) * LANES)
        x = conv_x[:, :, lanes].reshape(span, LANES)
        got = []
        for h in (2 * c, 2 * c + 1):
            halves = []
            for rows_of, width in ((slice(0, tokens), tokens), (slice(tokens, span), span)):
                gap = cols[rows_of, h : h + 1] - cumul[h : h + 1, :width]
                decays = jnp.exp(jnp.where(live[rows_of, :width], gap, -jnp.inf))
                mixing = (crossing[rows_of, :width] * decays * steps[h : h + 1, :width]).astype(BF16)
                halves.append(dot(mixing, x[:width], (1, 0)))
            got.append(jnp.concatenate(halves, axis=0))
        y_ref[:, lanes] = jnp.where(left, got[0], got[1])

    def attention():
        lax.fori_loop(1, me + 1, pass_on, 0)
        lax.fori_loop(0, me + 1, attend, 0)
        attended = (summed_ref[...] / total_ref[...]).astype(BF16)
        for h in range(heads_here):
            both[:, channels + h * HD : channels + (h + 1) * HD] = attended[h * tokens : (h + 1) * tokens]

    pl.when(me >= n_seq // 2)(attention)
    for c in range(chunks):
        lanes = slice(c * LANES, (c + 1) * LANES)

        @pl.when(has_lower)
        def _():
            for r in range(PIECES):
                i = PIECES * c + r
                e_hop(i, partner).wait_recv()

                @pl.when(has_upper)
                def _():
                    enters = e_recv[i].astype(F32)
                    e_send[i] = (through[:, lanes] * enters + state[r * depth : (r + 1) * depth, lanes]).astype(BF16)
                    e_hop(i, upper).start()

        enters = jnp.concatenate([e_recv[PIECES * c + r] for r in range(PIECES)], axis=0)
        carried = jnp.where(joined, two_heads(16, c), 0.0) * dot(read_c, enters, (1, 0))
        y = y_ref[:, lanes] + carried
        f_send[c] = jnp.where(on_left, y[tokens:], y[:tokens]).astype(BF16)
        f_hop(c).start()
        norm(side, c, gains[0], jnp.where(on_left, y[:tokens], y[tokens:]))

    pl.when(me < n_seq // 2)(attention)
    for c in range(chunks):
        f_hop(c).wait_recv()
        norm(other, c, gains[1], f_recv[c].astype(F32))

    for w in weights:
        w.wait()
    width = out_ref.shape[1]

    def product(j, part_of):
        at = pl.ds(pl.multiple_of(j * width + part_of * (width // 2), LANES), width // 2)
        return dot(both[:, :channels], mproj[:, at], (1, 0)) + dot(both[:, channels:], aproj[:, at], (1, 0))

    def rs_copy(i, target):
        return remote(rs_send.at[i], rs_recv.at[i], rs_ss.at[i], rs_rs.at[i], at_head(target))

    to_pair = [rs_copy(h, sibling) for h in range(2)]
    to_sibling = [rs_copy(2 + h, sibling) for h in range(2)]
    to_opposite = [rs_copy(4 + h, opposite) for h in range(2)]
    for h in range(2):
        rs_send[h] = product(opposite_sibling, h).astype(BF16)
        to_pair[h].start()
    for h in range(2):
        away = product(opposite, h)
        to_pair[h].wait_recv()
        rs_send[4 + h] = (away + rs_recv[h].astype(F32)).astype(BF16)
        to_opposite[h].start()
    for h in range(2):
        rs_send[2 + h] = product(sibling, h).astype(BF16)
        to_sibling[h].start()
    for h in range(2):
        result = product(mine, h)
        to_sibling[h].wait_recv()
        result = result + rs_recv[2 + h].astype(F32)
        to_opposite[h].wait_recv()
        out_ref[:, h * (width // 2) : (h + 1) * (width // 2)] = (result + rs_recv[4 + h].astype(F32)).astype(BF16)

    for copy in (*to_pair, *to_sibling, *to_opposite, group_copy(side), group_share(), step_copy(side)):
        copy.wait_send()
    for c in range(chunks):
        x_copy(side, c).wait_send()
        f_hop(c).wait_send()
    seg_copy(0, partner, 1 + side, 1 + side).wait_send()

    @pl.when(me < n_seq - 1)
    def _():
        for c in rim_next():
            c.wait_send()

    @pl.when(has_upper & (side == 1))
    def _():
        for c in rim_skip():
            c.wait_send()
        seg_copy(1, following, 2, 0).wait_send()
        seg_copy(2, upper, 2, 0).wait_send()

    @pl.when(has_upper)
    def _():
        for i in range(PIECES * chunks):
            e_hop(i, upper).wait_send()

    def sent_kv(k, _):
        kv_copy(me, k).wait_send()
        return 0

    lax.fori_loop(me + 1, n_seq, sent_kv, 0)

    def sent_share(d, _):
        kv_share(me - d).wait_send()
        return 0

    lax.fori_loop(1, me + 1, sent_share, 0)


def shards(n_seq, n_head, *arrays):
    (inner, groups, gate, step, bias, decay, taps_i, taps_g, gain, query, key, value, segs, mproj, aproj) = arrays
    tokens, channels = inner.shape
    half = channels // 2
    wide = groups.shape[1]
    out_width = mproj.shape[1] // n_head
    chunks = half // LANES
    vmem = pl.BlockSpec(memory_space=pltpu.VMEM)
    hbm = pl.BlockSpec(memory_space=pltpu.HBM)
    dma = pltpu.SemaphoreType.DMA
    scratch = [
        pltpu.VMEM(segs.shape, segs.dtype),
        pltpu.VMEM((2, *step.shape), F32),
        pltpu.VMEM(bias.shape, F32),
        pltpu.VMEM(decay.shape, F32),
        pltpu.VMEM((taps_i.shape[0], half), F32),
        pltpu.VMEM(taps_g.shape, F32),
        pltpu.VMEM(gain.shape, F32),
        pltpu.VMEM(query.shape, BF16),
        pltpu.VMEM(gate.shape, BF16),
        pltpu.VMEM((2, tokens, half), BF16),
        pltpu.VMEM((2, tokens, wide), BF16),
        pltpu.VMEM((2, RIM, half), BF16),
        pltpu.VMEM((2, RIM, wide), BF16),
        pltpu.VMEM((3, RIM, tokens), BF16),
        pltpu.VMEM((n_seq, 2, tokens + RIM, HD), BF16),
        pltpu.VMEM((2, RIM + tokens, half), F32),
        pltpu.VMEM((2, RIM + tokens, wide), F32),
        pltpu.VMEM((2, tokens, half), BF16),
        pltpu.VMEM((2, tokens, STATE_SIZE), BF16),
        pltpu.VMEM((2, tokens, STATE_SIZE), BF16),
        pltpu.VMEM((2 * tokens, half), F32),
        pltpu.VMEM((STATE_SIZE, half), F32),
        *[pltpu.VMEM((PIECES * chunks, STATE_SIZE // PIECES, LANES), BF16) for _ in range(2)],
        *[pltpu.VMEM((chunks, tokens, LANES), BF16) for _ in range(2)],
        pltpu.VMEM((tokens, channels + query.shape[1]), BF16),
        pltpu.VMEM(mproj.shape, BF16),
        pltpu.VMEM(aproj.shape, BF16),
        pltpu.VMEM((6, tokens, out_width // 2), BF16),
        pltpu.VMEM((6, tokens, out_width // 2), BF16),
        *[pltpu.VMEM((query.shape[1] // HD * tokens, n), F32) for n in (1, 1, HD)],
        pltpu.SemaphoreType.REGULAR((n_seq,)),
        dma((13,)),
        dma((2,)),
        dma((chunks,)),
        dma((chunks,)),
        dma((2,)),
        dma((2,)),
        dma((2,)),
        dma((2, 2)),
        dma((2, 2)),
        dma((3,)),
        dma((3,)),
        *[dma((n_seq,)) for _ in range(4)],
        *[dma((PIECES * chunks,)) for _ in range(2)],
        *[dma((chunks,)) for _ in range(2)],
        dma((6,)),
        dma((6,)),
    ]
    return pl.pallas_call(
        functools.partial(kernel, n_seq, n_head),
        out_shape=jax.ShapeDtypeStruct((tokens, out_width), BF16),
        in_specs=[hbm] * 15,
        out_specs=vmem,
        scratch_shapes=scratch,
        compiler_params=pltpu.CompilerParams(
            collective_id=0, has_side_effects=True, vmem_limit_bytes=64 * 2**20
        ),
        name="mixer",
    )(*arrays)


def solution(mesh):
    placed = (
        P("seq", "head"),
        P("seq", None),
        P("seq", "head"),
        P("head", "seq"),
        P("head"),
        P("head"),
        P(None, "head"),
        P(),
        P("head"),
        P("seq", "head"),
        P("seq", None),
        P("seq", None),
        P("seq"),
        P("head", None),
        P("head", None),
    )
    return jax.shard_map(
        functools.partial(shards, mesh.shape["seq"], mesh.shape["head"]),
        mesh=mesh,
        in_specs=placed,
        out_specs=P("seq", "head"),
        check_vma=False,
    )
```

time: 37.4 us -> 33.7 us (0.901); the launches traced: 36.7 us -> 33.6 us
  Pallas kernels: 35.1 us -> 32 us
    pallas_call x1, Pallas kernels: 35.1 us -> 32 us  [shards(): pl.pallas_call(functools.partial(kernel, n_seq, n_head), out_shape=jax.Sh...]
where the time goes in v1:
time: 33.7 us; the launch traced here: 33.6 us
  Pallas kernels  32 us (95%)
  local copies, waits for them, and re-layouts  1.57 us (5%)
    pallas_call x1, Pallas kernels, shards(): pl.pallas_call(functools.partial(kernel, n_seq, n_head), out_shape=jax.Sh...  32 us
    unnamed x1, local copies, waits for them, and re-layouts  1.57 us

profile of v1, /device:TPU:25, one launch (start us, length us, event | category | flops | bytes accessed | tf_op | source)
XLA Modules:
  0.0 33.6 jit_solution(13685503888215952934)
XLA Ops:
  0.0 32.0 %mixer.1 = bf16[128,512]{1,0:T(8,128)(2,1)} custom-call(bf16[128,768]{1,0:T(8,128)(2,1)} %inner_hbm.1, bf16[128,512]{1,0:T(8,128)(2,1)} %groups_hbm.1, bf16[128,768]{1,0:T(8,128)(2,1)} %gate_hbm.1, f32[12,128]{1,0:T(8,128)} %step_hbm.1, f32[12]{0:T(128)} %bias_hbm.1, f32[12]{0:T(128)} %decay_hbm.1, f32[4,768]{1,0:T(4,128)} %taps_inner_hbm.1, ...), custom_call_target="tpu_custom_call" | custom-call | tf_op jit(solution)/shard_map/mixer/pallas_call | solution.py:706
  32.0 1.6 %copy.17 = bf16[128,512]{1,0:T(8,128)(2,1)} copy(bf16[128,512]{1,0:T(8,128)(2,1)} %mixer.1) | data formatting | bytes 262144

commit v2 on v1

--- a/solution.py
+++ b/solution.py
@@ -80,7 +80,6 @@
     g_in,
     rim_x,
     rim_g,
-    segt,
     kv,
     pad_x,
     pad_g,
@@ -114,6 +113,7 @@
     seg_ss,
     seg_rs,
     kv_ss,
+    across_ss,
     kv_rs,
     share_ss,
     share_rs,
@@ -164,7 +164,9 @@
     def side_half(which):
         return pl.ds(pl.multiple_of(which * half, LANES), half)
 
-    core_cols = pl.ds(pl.multiple_of(core * STATE_SIZE, STATE_SIZE), STATE_SIZE)
+    def core_cols(kind):
+        return pl.ds(pl.multiple_of(kind * STATE_SIZE + core * LANES, LANES), LANES)
+
     kv_head = mine * heads_here // (QH // KVH)
     kv_cols = pl.ds(pl.multiple_of(kv_head * HD, HD), HD)
     body = pl.ds(0, tokens)
@@ -177,7 +179,7 @@
         pltpu.make_async_copy(src, dst, load_sem.at[i])
         for i, (src, dst) in enumerate(
             (
-                (segs_hbm, segs_ref),
+                (segs_hbm, segs_ref.at[1 + side, 0]),
                 (key_hbm.at[:, kv_cols], kv.at[me, 0, body]),
                 (value_hbm.at[:, kv_cols], kv.at[me, 1, body]),
                 (groups_hbm, g_in.at[side]),
@@ -203,20 +205,28 @@
     hello(at_head(sibling))
     hello(at_head(opposite))
 
-    def hello_later(k, _):
-        hello(at_seq(k))
+    def hello_later(s, _):
+        hello(at_seq(me + 2 * s))
         return 0
 
-    lax.fori_loop(2 * pair + 2, n_seq, hello_later, 0)
+    lax.fori_loop(1, last_pair - pair + 1, hello_later, 0)
+
+    @pl.when(has_upper & (side == 1))
+    def _():
+        hello(at_seq(following))
+
     for w in loads:
         w.start()
-    pl.semaphore_wait(barrier, 3 + 2 * pair)
-
-    def answer(k, _):
+    pl.semaphore_wait(barrier, 3 + pair + jnp.where(has_lower, other, 0))
+
+    def answer(k):
         pl.semaphore_signal(ready.at[me], inc=1, device_id=at_seq(k), device_id_type=MESH)
-        return 0
-
-    lax.fori_loop(0, 2 * pair, answer, 0)
+
+    @pl.when(has_lower & (side == 0))
+    def _():
+        answer(previous)
+
+    lax.fori_loop(1, pair + 1, lambda s, _: answer(me - 2 * s) or 0, 0)
 
     tail_rows = pl.ds(tokens - RIM, RIM)
 
@@ -234,15 +244,13 @@
     def rim_skip():
         return rim_copies(1, upper, 0, side)
 
-    def group_copy(block):
-        return remote(
-            groups_hbm.at[:, core_cols], g_in.at[block, :, core_cols], g_ss.at[0], g_rs.at[0], at_seq(partner)
-        )
-
-    def group_share():
-        return remote(
-            g_in.at[other, :, core_cols], g_in.at[other, :, core_cols], g_ss.at[1], g_rs.at[1], at_head(sibling)
-        )
+    def group_copy(block, kind):
+        at = core_cols(kind)
+        return remote(groups_hbm.at[:, at], g_in.at[block, :, at], g_ss.at[kind], g_rs.at[kind], at_seq(partner))
+
+    def group_share(kind):
+        at = core_cols(kind)
+        return remote(g_in.at[other, :, at], g_in.at[other, :, at], g_ss.at[2 + kind], g_rs.at[2 + kind], at_head(sibling))
 
     def x_copy(block, c):
         return remote(
@@ -256,24 +264,23 @@
     def step_copy(block):
         return remote(step_hbm, step_in.at[block], step_sem.at[0], step_sem.at[1], at_seq(partner))
 
-    loads[0].wait()
-    own_segs = jnp.broadcast_to(segs_ref[...].reshape(1, tokens).astype(F32), (RIM, tokens)).astype(BF16)
-    segt[1 + side] = own_segs
-
-    def seg_copy(kind, target, src, dst):
-        return remote(segt.at[src], segt.at[dst], seg_ss.at[kind], seg_rs.at[dst], at_seq(target))
+    def seg_copy(kind, target, dst):
+        return remote(segs_hbm, segs_ref.at[dst, 0], seg_ss.at[kind], seg_rs.at[dst], at_seq(target))
 
     step_copy(side).start()
-    seg_copy(0, partner, 1 + side, 1 + side).start()
+    seg_copy(0, partner, 1 + side).start()
+
+    group_copy(side, 0).start()
+    x_copy(side, 0).start()
 
     @pl.when(side == 0)
     def _():
         for c in rim_next():
             c.start()
 
-    group_copy(side).start()
-    for c in range(chunks):
+    for c in range(1, chunks):
         x_copy(side, c).start()
+    group_copy(side, 1).start()
 
     def kv_copy(b, k):
         return remote(kv.at[b, core], kv.at[b, core], kv_ss.at[k], kv_rs.at[b], at_seq(k))
@@ -281,13 +288,22 @@
     def kv_share(b):
         return remote(kv.at[b, core], kv.at[b, core], share_ss.at[b], share_rs.at[b], at_head(sibling))
 
-    def pass_on(d, _):
-        kv_copy(me - d, partner).wait_recv()
-        kv_share(me - d).start()
+    def kv_across(b):
+        return remote(kv.at[b, core], kv.at[b, core], across_ss.at[b], kv_rs.at[b], at_seq(partner))
+
+    def pass_on(s, _):
+        kv_copy(me - 2 * s, partner).wait_recv()
+        kv_across(me - 2 * s).start()
+        kv_share(me - 2 * s).start()
         return 0
 
+    def pass_across(s, _):
+        kv_across(partner - 2 * s).wait_recv()
+        kv_share(partner - 2 * s).start()
+        return 0
+
     def conv_flags(b, before):
-        now = segt[b + 1].astype(F32)[0:8]
+        now = segs_of(b + 1)
         both_blocks = jnp.concatenate([before, now], axis=1)
         row = iota((8, tokens), 0)
         flags = now
@@ -308,11 +324,11 @@
             acc = acc + jnp.where(keeps[k], term, 0.0)
         return jax.nn.silu(acc).astype(BF16)
 
-    def conv_groups(b, keeps, n):
-        for out, base in ((conv_b, 0), (conv_c, STATE_SIZE)):
-            for c in range(0, STATE_SIZE, LANES):
-                at = slice(base + c, base + c + LANES)
-                out[b, 0:n, c : c + LANES] = conv(pad_g, b, at, keeps, taps_groups_ref, n)
+    def conv_groups(b, kind, keeps, n):
+        out = (conv_b, conv_c)[kind]
+        for c in range(0, STATE_SIZE, LANES):
+            at = slice(kind * STATE_SIZE + c, kind * STATE_SIZE + c + LANES)
+            out[b, 0:n, c : c + LANES] = conv(pad_g, b, at, keeps, taps_groups_ref, n)
 
     def conv_inner(b, c, keeps, n):
         at = slice(c * LANES, (c + 1) * LANES)
@@ -322,7 +338,10 @@
         for c in rim_copies(0, partner, slot, slot):
             c.wait_recv()
 
-    for w in loads[3:7]:
+    def segs_of(at):
+        return jnp.broadcast_to(segs_ref[at].astype(F32), (8, tokens))
+
+    for w in (loads[0], *loads[3:7]):
         w.wait()
     pad_g[side, 0:RIM, :] = jnp.zeros((RIM, wide), F32)
     pad_x[side, 0:RIM, :] = jnp.zeros((RIM, half), F32)
@@ -330,8 +349,10 @@
     pad_x[side, RIM:, :] = x_in[side].astype(F32)
     own_flags = conv_flags(side, jnp.full((8, tokens), -1.0, F32))
     own_keeps = keeps_of(own_flags, tokens)
-    conv_groups(side, own_keeps, tokens)
-
+    conv_groups(side, 0, own_keeps, tokens)
+    conv_groups(side, 1, own_keeps, tokens)
+
+    own_segs = jnp.broadcast_to(segs_ref[1 + side].astype(F32), (RIM, tokens)).astype(BF16)
     kv[me, 0, pl.ds(tokens, RIM), :] = own_segs
     kv[me, 1, pl.ds(tokens, RIM), :] = own_segs
     loads[1].wait()
@@ -339,7 +360,7 @@
 
     @pl.when(side == 0)
     def _():
-        kv_copy(me, partner).start()
+        kv_across(me).start()
 
     @pl.when(has_upper)
     def _():
@@ -348,13 +369,12 @@
     @pl.when(has_upper & (side == 1))
     def _():
         pl.semaphore_wait(ready.at[following], 1)
-        seg_copy(1, following, 2, 0).start()
-        seg_copy(2, upper, 2, 0).start()
+        seg_copy(1, following, 0).start()
+        seg_copy(2, upper, 0).start()
         for c in rim_skip():
             c.start()
         for c in rim_next():
             c.start()
-        kv_copy(me, following).start()
 
     @pl.when(has_upper)
     def _():
@@ -366,7 +386,7 @@
     for w in loads[7:10]:
         w.wait()
     step_copy(other).wait_recv()
-    seg_copy(0, partner, 1 + other, 1 + other).wait_recv()
+    seg_copy(0, partner, 1 + other).wait_recv()
     bias = column(bias_ref[...].reshape(1, heads))
     rates = jnp.exp(column(decay_ref[...].reshape(1, heads)))
     on_left = side == 0
@@ -383,7 +403,7 @@
     sums = dot(thirds(-steps * mine_of(rates)), upto, (1, 0))
     cumul = sums[0:8] + sums[8:16] + sums[16:24]
     total = cumul[:, span - 1 : span]
-    segs_rows8 = jnp.concatenate([segt[1].astype(F32)[0:8], segt[2].astype(F32)[0:8]], axis=1)
+    segs_rows8 = jnp.concatenate([segs_of(1), segs_of(2)], axis=1)
     last_seg = segs_rows8[:, span - 1 : span]
     weigh = jnp.where(segs_rows8 == last_seg, jnp.exp(total - cumul), 0.0) * steps
     cols = to_columns(jnp.concatenate([cumul, weigh, jnp.exp(cumul), segs_rows8], axis=0))
@@ -393,17 +413,39 @@
         a, b = base + 2 * c, base + 2 * c + 1
         return jnp.where(left, cols[:, a : a + 1], cols[:, b : b + 1])
 
-    group_copy(other).wait_recv()
-    group_share().start()
+    group_copy(other, 0).wait_recv()
+    group_share(0).start()
+
+    def send_far(s, _):
+        pl.semaphore_wait(ready.at[me + 2 * s], 1)
+        kv_copy(me, me + 2 * s).start()
+        return 0
+
+    lax.fori_loop(2, last_pair - pair + 1, send_far, 0)
+
+    other_keeps = keeps_of(conv_flags(other, jnp.full((8, tokens), -1.0, F32)), tokens)
+    pad_g[other, 0:RIM, :] = jnp.zeros((RIM, wide), F32)
+    pad_x[other, 0:RIM, :] = jnp.zeros((RIM, half), F32)
+    group_share(0).wait_recv()
+    pad_g[other, RIM:, 0:STATE_SIZE] = g_in[other, :, 0:STATE_SIZE].astype(F32)
+    conv_groups(other, 0, other_keeps, tokens)
+
+    def conv_other(c):
+        lanes = slice(c * LANES, (c + 1) * LANES)
+        x_copy(other, c).wait_recv()
+        pad_x[other, RIM:, lanes] = x_in[other, :, lanes].astype(F32)
+        conv_inner(other, c, other_keeps, tokens)
+
+    conv_other(0)
 
     @pl.when(has_lower)
     def _():
-        seg_copy(0, partner, 0, 0).wait_recv()
+        seg_copy(0, partner, 0).wait_recv()
         rim_arrived(0)
 
     @pl.when(pair == 0)
     def _():
-        segt[0] = jnp.full((RIM, tokens), -1.0, BF16)
+        segs_ref[0] = jnp.full((1, tokens), -1, jnp.int32)
         rim_x[0] = jnp.zeros_like(rim_x[0])
         rim_g[0] = jnp.zeros_like(rim_g[0])
 
@@ -416,32 +458,15 @@
         rim_x[1] = x_in[0, tokens - RIM :, :]
         rim_g[1] = g_in[0, tokens - RIM :, :]
 
+    first_keeps = []
     for b in range(2):
         pad_g[b, 0:RIM, :] = rim_g[b].astype(F32)
         pad_x[b, 0:RIM, :] = rim_x[b].astype(F32)
-    first_keeps = keeps_of(conv_flags(side, segt[side].astype(F32)[0:8]), RIM)
-    conv_groups(side, first_keeps, RIM)
-    for c in range(chunks):
-        conv_inner(side, c, first_keeps, RIM)
-    prev_last = segt[0].astype(F32)[0:8, tokens - 1 : tokens]
-    spread = iota((8, half), 1) // HEAD_CHANNELS == iota((8, half), 0)
-    crossing_pair = jnp.where(last_seg == prev_last, jnp.exp(total), 0.0)
-    through = jnp.sum(jnp.where(spread, crossing_pair, 0.0), axis=0, keepdims=True)
-    joined = cols[:, 24:25] == prev_last[0:1]
-
-    def send_far(k, _):
-        pl.semaphore_wait(ready.at[k], 1)
-        kv_copy(me, k).start()
-        return 0
-
-    lax.fori_loop(me + 3, n_seq, send_far, 0)
-
-    other_keeps = keeps_of(conv_flags(other, segt[other].astype(F32)[0:8]), tokens)
-    group_share().wait_recv()
-    pad_g[other, RIM:, :] = g_in[other].astype(F32)
-    conv_groups(other, other_keeps, tokens)
+        first_keeps.append(keeps_of(conv_flags(b, segs_of(b)), RIM))
+        conv_groups(b, 0, first_keeps[b], RIM)
+
     read_b = conv_b[...].reshape(span, STATE_SIZE)
-    read_c = conv_c[...].reshape(span, STATE_SIZE)
+    across_b = read_b.T
 
     def hop(src, dst, ss, rs, c, target):
         return remote(src.at[c], dst.at[c], ss.at[c], rs.at[c], at_seq(target))
@@ -450,12 +475,13 @@
         return hop(e_send, e_recv, e_ss, e_rs, i, target)
 
     for c in range(chunks):
-        x_copy(other, c).wait_recv()
+        if c > 0:
+            conv_other(c)
+        for b in range(2):
+            conv_inner(b, c, first_keeps[b], RIM)
         lanes = slice(c * LANES, (c + 1) * LANES)
-        pad_x[other, RIM:, lanes] = x_in[other, :, lanes].astype(F32)
-        conv_inner(other, c, other_keeps, tokens)
         x = conv_x[:, :, lanes].reshape(span, LANES).astype(F32)
-        state[:, lanes] = dot(read_b, (two_heads(8, c) * x).astype(BF16), (0, 0))
+        state[:, lanes] = dot(across_b, (two_heads(8, c) * x).astype(BF16), (1, 0))
 
         @pl.when(pair == 0)
         def _():
@@ -464,8 +490,25 @@
                 e_send[i] = state[r * depth : (r + 1) * depth, lanes].astype(BF16)
                 e_hop(i, upper).start()
 
+    group_copy(other, 1).wait_recv()
+    group_share(1).start()
+
+    prev_last = segs_of(0)[:, tokens - 1 : tokens]
+    spread = iota((8, half), 1) // HEAD_CHANNELS == iota((8, half), 0)
+    crossing_pair = jnp.where(last_seg == prev_last, jnp.exp(total), 0.0)
+    through = jnp.sum(jnp.where(spread, crossing_pair, 0.0), axis=0, keepdims=True)
+    joined = cols[:, 24:25] == prev_last[0:1]
+    group_share(1).wait_recv()
+    pad_g[other, RIM:, STATE_SIZE:] = g_in[other, :, STATE_SIZE:].astype(F32)
+    conv_groups(other, 1, other_keeps, tokens)
+    for b in range(2):
+        conv_groups(b, 1, first_keeps[b], RIM)
+    read_c = conv_c[...].reshape(span, STATE_SIZE)
+
     for w in weights:
         w.start()
+
+    lax.fori_loop(1, pair + 1, pass_on, 0)
 
     for w in loads[10:]:
         w.wait()
@@ -478,10 +521,8 @@
     total_ref[...] = jnp.zeros((rows, 1), F32)
     summed_ref[...] = jnp.zeros((rows, HD), F32)
 
-    def attend(d, _):
-        k = me - d
-
-        @pl.when(d > 0)
+    def attend(k):
+        @pl.when(k != me)
         def _():
             kv_share(k).wait_recv()
 
@@ -496,7 +537,6 @@
         top_ref[...] = new_top
         total_ref[...] = total_ref[...] * rescale + jnp.sum(w, axis=1, keepdims=True)
         summed_ref[...] = summed_ref[...] * rescale + dot(w.astype(BF16), kv[k, 1, 0:tokens, :], (1, 0))
-        return 0
 
     same_head = (iota((2 * LANES, LANES), 0) % LANES // HEAD_CHANNELS == iota((2 * LANES, LANES), 1) // HEAD_CHANNELS).astype(
         BF16
@@ -525,7 +565,7 @@
         e_recv[...] = jnp.zeros_like(e_recv)
 
     live = (cols[:, 24:25] == segs_rows8[0:1]) & (row_t >= col_t)
-    crossing = dot(read_c, read_b, (1, 1))
+    crossing = dot(read_c, across_b, (1, 0))
     for c in range(chunks):
         lanes = slice(c * LANES, (c + 1) * LANES)
         x = conv_x[:, :, lanes].reshape(span, LANES)
@@ -541,13 +581,14 @@
         y_ref[:, lanes] = jnp.where(left, got[0], got[1])
 
     def attention():
-        lax.fori_loop(1, me + 1, pass_on, 0)
-        lax.fori_loop(0, me + 1, attend, 0)
+        lax.fori_loop(0, pair + 1, lambda s, _: attend(me - 2 * s) or 0, 0)
+        lax.fori_loop(other, pair + 1, pass_across, 0)
+        lax.fori_loop(other, pair + 1, lambda s, _: attend(partner - 2 * s) or 0, 0)
         attended = (summed_ref[...] / total_ref[...]).astype(BF16)
         for h in range(heads_here):
             both[:, channels + h * HD : channels + (h + 1) * HD] = attended[h * tokens : (h + 1) * tokens]
 
-    pl.when(me >= n_seq // 2)(attention)
+    pl.when(pair == last_pair)(attention)
     for c in range(chunks):
         lanes = slice(c * LANES, (c + 1) * LANES)
 
@@ -570,7 +611,7 @@
         f_hop(c).start()
         norm(side, c, gains[0], jnp.where(on_left, y[:tokens], y[tokens:]))
 
-    pl.when(me < n_seq // 2)(attention)
+    pl.when(pair < last_pair)(attention)
     for c in range(chunks):
         f_hop(c).wait_recv()
         norm(other, c, gains[1], f_recv[c].astype(F32))
@@ -607,12 +648,15 @@
         to_opposite[h].wait_recv()
         out_ref[:, h * (width // 2) : (h + 1) * (width // 2)] = (result + rs_recv[4 + h].astype(F32)).astype(BF16)
 
-    for copy in (*to_pair, *to_sibling, *to_opposite, group_copy(side), group_share(), step_copy(side)):
+    for copy in (*to_pair, *to_sibling, *to_opposite, step_copy(side)):
         copy.wait_send()
     for c in range(chunks):
         x_copy(side, c).wait_send()
         f_hop(c).wait_send()
-    seg_copy(0, partner, 1 + side, 1 + side).wait_send()
+    for kind in range(2):
+        group_copy(side, kind).wait_send()
+        group_share(kind).wait_send()
+    seg_copy(0, partner, 1 + side).wait_send()
 
     @pl.when(me < n_seq - 1)
     def _():
@@ -623,25 +667,36 @@
     def _():
         for c in rim_skip():
             c.wait_send()
-        seg_copy(1, following, 2, 0).wait_send()
-        seg_copy(2, upper, 2, 0).wait_send()
+        seg_copy(1, following, 0).wait_send()
+        seg_copy(2, upper, 0).wait_send()
 
     @pl.when(has_upper)
     def _():
         for i in range(PIECES * chunks):
             e_hop(i, upper).wait_send()
 
-    def sent_kv(k, _):
-        kv_copy(me, k).wait_send()
+    def sent_kv(s, _):
+        kv_copy(me, me + 2 * s).wait_send()
         return 0
 
-    lax.fori_loop(me + 1, n_seq, sent_kv, 0)
-
-    def sent_share(d, _):
-        kv_share(me - d).wait_send()
+    lax.fori_loop(1, last_pair - pair + 1, sent_kv, 0)
+
+    def sent_on(s, _):
+        kv_across(me - 2 * s).wait_send()
+        kv_share(me - 2 * s).wait_send()
         return 0
 
-    lax.fori_loop(1, me + 1, sent_share, 0)
+    lax.fori_loop(1, pair + 1, sent_on, 0)
+
+    @pl.when(side == 0)
+    def _():
+        kv_across(me).wait_send()
+
+    def sent_share(s, _):
+        kv_share(partner - 2 * s).wait_send()
+        return 0
+
+    lax.fori_loop(other, pair + 1, sent_share, 0)
 
 
 def shards(n_seq, n_head, *arrays):
@@ -655,7 +710,7 @@
     hbm = pl.BlockSpec(memory_space=pltpu.HBM)
     dma = pltpu.SemaphoreType.DMA
     scratch = [
-        pltpu.VMEM(segs.shape, segs.dtype),
+        pltpu.VMEM((3, 1, tokens), segs.dtype),
         pltpu.VMEM((2, *step.shape), F32),
         pltpu.VMEM(bias.shape, F32),
         pltpu.VMEM(decay.shape, F32),
@@ -668,7 +723,6 @@
         pltpu.VMEM((2, tokens, wide), BF16),
         pltpu.VMEM((2, RIM, half), BF16),
         pltpu.VMEM((2, RIM, wide), BF16),
-        pltpu.VMEM((3, RIM, tokens), BF16),
         pltpu.VMEM((n_seq, 2, tokens + RIM, HD), BF16),
         pltpu.VMEM((2, RIM + tokens, half), F32),
         pltpu.VMEM((2, RIM + tokens, wide), F32),
@@ -690,14 +744,14 @@
         dma((2,)),
         dma((chunks,)),
         dma((chunks,)),
-        dma((2,)),
-        dma((2,)),
+        dma((4,)),
+        dma((4,)),
         dma((2,)),
         dma((2, 2)),
         dma((2, 2)),
         dma((3,)),
         dma((3,)),
-        *[dma((n_seq,)) for _ in range(4)],
+        *[dma((n_seq,)) for _ in range(5)],
         *[dma((PIECES * chunks,)) for _ in range(2)],
         *[dma((chunks,)) for _ in range(2)],
         dma((6,)),

time: 33.7 us -> 31.5 us (0.935)
  Pallas kernels: 32 us -> 29.8 us
    pallas_call x1, Pallas kernels: 32 us -> 29.8 us  [shards(): pl.pallas_call(functools.partial(kernel, n_seq, n_head), out_shape=jax.Sh...]
where the time goes in v2:
time: 31.5 us; the launch traced here: 31.3 us
  Pallas kernels  29.8 us (95%)
  local copies, waits for them, and re-layouts  1.57 us (5%)
    pallas_call x1, Pallas kernels, shards(): pl.pallas_call(functools.partial(kernel, n_seq, n_head), out_shape=jax.Sh...  29.8 us
    unnamed x1, local copies, waits for them, and re-layouts  1.57 us

profile of v2, /device:TPU:25, one launch (start us, length us, event | category | flops | bytes accessed | tf_op | source)
XLA Modules:
  0.0 31.3 jit_solution(10379471991997308922)
XLA Ops:
  0.0 29.8 %mixer.1 = bf16[128,512]{1,0:T(8,128)(2,1)} custom-call(bf16[128,768]{1,0:T(8,128)(2,1)} %inner_hbm.1, bf16[128,512]{1,0:T(8,128)(2,1)} %groups_hbm.1, bf16[128,768]{1,0:T(8,128)(2,1)} %gate_hbm.1, f32[12,128]{1,0:T(8,128)} %step_hbm.1, f32[12]{0:T(128)} %bias_hbm.1, f32[12]{0:T(128)} %decay_hbm.1, f32[4,768]{1,0:T(4,128)} %taps_inner_hbm.1, ...), custom_call_target="tpu_custom_call" | custom-call | tf_op jit(solution)/shard_map/mixer/pallas_call | solution.py:760
  29.8 1.6 %copy.17 = bf16[128,512]{1,0:T(8,128)(2,1)} copy(bf16[128,512]{1,0:T(8,128)(2,1)} %mixer.1) | data formatting | bytes 262144

commit v3 on v2

--- a/solution.py
+++ b/solution.py
@@ -97,6 +97,7 @@
     aproj,
     rs_send,
     rs_recv,
+    scores_ref,
     top_ref,
     total_ref,
     summed_ref,
@@ -350,7 +351,6 @@
     own_flags = conv_flags(side, jnp.full((8, tokens), -1.0, F32))
     own_keeps = keeps_of(own_flags, tokens)
     conv_groups(side, 0, own_keeps, tokens)
-    conv_groups(side, 1, own_keeps, tokens)
 
     own_segs = jnp.broadcast_to(segs_ref[1 + side].astype(F32), (RIM, tokens)).astype(BF16)
     kv[me, 0, pl.ds(tokens, RIM), :] = own_segs
@@ -492,6 +492,9 @@
 
     group_copy(other, 1).wait_recv()
     group_share(1).start()
+    pad_g[side, 0:RIM, STATE_SIZE:] = jnp.zeros((RIM, STATE_SIZE), F32)
+    conv_groups(side, 1, own_keeps, tokens)
+    pad_g[side, 0:RIM, STATE_SIZE:] = rim_g[side, :, STATE_SIZE:].astype(F32)
 
     prev_last = segs_of(0)[:, tokens - 1 : tokens]
     spread = iota((8, half), 1) // HEAD_CHANNELS == iota((8, half), 0)
@@ -517,8 +520,8 @@
     rows = heads_here * tokens
     segs_q = jnp.concatenate([own_flags[:, 0:1]] * heads_here, axis=0)
     token_q = jnp.concatenate([iota((tokens, 1), 0)] * heads_here, axis=0)
-    top_ref[...] = jnp.full((rows, 1), -1e30, F32)
-    total_ref[...] = jnp.zeros((rows, 1), F32)
+    top_ref[...] = jnp.full((rows, tokens), -jnp.inf, F32)
+    total_ref[...] = jnp.zeros((rows, tokens), F32)
     summed_ref[...] = jnp.zeros((rows, HD), F32)
 
     def attend(k):
@@ -530,13 +533,8 @@
         segs_k = kv[k, 0, tokens:, :].astype(F32)[0:1, :tokens]
         allowed = (segs_k == segs_q) & (iota((rows, tokens), 1) + (k - me) * tokens <= token_q)
         scores = jnp.where(allowed, scores, -jnp.inf)
-        top = top_ref[...]
-        new_top = jnp.maximum(top, jnp.max(scores, axis=1, keepdims=True))
-        rescale = jnp.exp(top - new_top)
-        w = jnp.exp(scores - new_top)
-        top_ref[...] = new_top
-        total_ref[...] = total_ref[...] * rescale + jnp.sum(w, axis=1, keepdims=True)
-        summed_ref[...] = summed_ref[...] * rescale + dot(w.astype(BF16), kv[k, 1, 0:tokens, :], (1, 0))
+        scores_ref[k] = scores
+        top_ref[...] = jnp.maximum(top_ref[...], scores)
 
     same_head = (iota((2 * LANES, LANES), 0) % LANES // HEAD_CHANNELS == iota((2 * LANES, LANES), 1) // HEAD_CHANNELS).astype(
         BF16
@@ -580,15 +578,26 @@
             got.append(jnp.concatenate(halves, axis=0))
         y_ref[:, lanes] = jnp.where(left, got[0], got[1])
 
-    def attention():
+    def attend_line():
         lax.fori_loop(0, pair + 1, lambda s, _: attend(me - 2 * s) or 0, 0)
         lax.fori_loop(other, pair + 1, pass_across, 0)
+
+    def attend_rest():
         lax.fori_loop(other, pair + 1, lambda s, _: attend(partner - 2 * s) or 0, 0)
-        attended = (summed_ref[...] / total_ref[...]).astype(BF16)
+        top = jnp.max(top_ref[...], axis=1, keepdims=True)
+
+        def add(k, _):
+            w = jnp.exp(scores_ref[k] - top)
+            total_ref[...] += w
+            summed_ref[...] += dot(w.astype(BF16), kv[k, 1, 0:tokens, :], (1, 0))
+            return 0
+
+        lax.fori_loop(0, me + 1, add, 0)
+        attended = (summed_ref[...] / jnp.sum(total_ref[...], axis=1, keepdims=True)).astype(BF16)
         for h in range(heads_here):
             both[:, channels + h * HD : channels + (h + 1) * HD] = attended[h * tokens : (h + 1) * tokens]
 
-    pl.when(pair == last_pair)(attention)
+    pl.when(pair == last_pair)(attend_line)
     for c in range(chunks):
         lanes = slice(c * LANES, (c + 1) * LANES)
 
@@ -611,7 +620,8 @@
         f_hop(c).start()
         norm(side, c, gains[0], jnp.where(on_left, y[:tokens], y[tokens:]))
 
-    pl.when(pair < last_pair)(attention)
+    pl.when(pair < last_pair)(attend_line)
+    attend_rest()
     for c in range(chunks):
         f_hop(c).wait_recv()
         norm(other, c, gains[1], f_recv[c].astype(F32))
@@ -738,7 +748,8 @@
         pltpu.VMEM(aproj.shape, BF16),
         pltpu.VMEM((6, tokens, out_width // 2), BF16),
         pltpu.VMEM((6, tokens, out_width // 2), BF16),
-        *[pltpu.VMEM((query.shape[1] // HD * tokens, n), F32) for n in (1, 1, HD)],
+        pltpu.VMEM((n_seq, query.shape[1] // HD * tokens, tokens), F32),
+        *[pltpu.VMEM((query.shape[1] // HD * tokens, n), F32) for n in (tokens, tokens, HD)],
         pltpu.SemaphoreType.REGULAR((n_seq,)),
         dma((13,)),
         dma((2,)),

time: 31.5 us -> 31.4 us (level)
  no operation moved by 1% of the time
where the time goes in v3:
time: 31.4 us; the launch traced here: 31.3 us
  Pallas kernels  29.7 us (95%)
  local copies, waits for them, and re-layouts  1.57 us (5%)
    pallas_call x1, Pallas kernels, shards(): pl.pallas_call(functools.partial(kernel, n_seq, n_head), out_shape=jax.Sh...  29.7 us
    unnamed x1, local copies, waits for them, and re-layouts  1.57 us

profile of v3, /device:TPU:25, one launch (start us, length us, event | category | flops | bytes accessed | tf_op | source)
XLA Modules:
  0.0 31.3 jit_solution(2522590946663256151)
XLA Ops:
  0.0 29.7 %mixer.1 = bf16[128,512]{1,0:T(8,128)(2,1)} custom-call(bf16[128,768]{1,0:T(8,128)(2,1)} %inner_hbm.1, bf16[128,512]{1,0:T(8,128)(2,1)} %groups_hbm.1, bf16[128,768]{1,0:T(8,128)(2,1)} %gate_hbm.1, f32[12,128]{1,0:T(8,128)} %step_hbm.1, f32[12]{0:T(128)} %bias_hbm.1, f32[12]{0:T(128)} %decay_hbm.1, f32[4,768]{1,0:T(4,128)} %taps_inner_hbm.1, ...), custom_call_target="tpu_custom_call" | custom-call | tf_op jit(solution)/shard_map/mixer/pallas_call | solution.py:771
  29.7 1.6 %copy.17 = bf16[128,512]{1,0:T(8,128)(2,1)} copy(bf16[128,512]{1,0:T(8,128)(2,1)} %mixer.1) | data formatting | bytes 262144

commit v4 on v3

--- a/solution.py
+++ b/solution.py
@@ -166,7 +166,7 @@
         return pl.ds(pl.multiple_of(which * half, LANES), half)
 
     def core_cols(kind):
-        return pl.ds(pl.multiple_of(kind * STATE_SIZE + core * LANES, LANES), LANES)
+        return pl.ds(kind * STATE_SIZE, STATE_SIZE)
 
     kv_head = mine * heads_here // (QH // KVH)
     kv_cols = pl.ds(pl.multiple_of(kv_head * HD, HD), HD)
@@ -249,10 +249,6 @@
         at = core_cols(kind)
         return remote(groups_hbm.at[:, at], g_in.at[block, :, at], g_ss.at[kind], g_rs.at[kind], at_seq(partner))
 
-    def group_share(kind):
-        at = core_cols(kind)
-        return remote(g_in.at[other, :, at], g_in.at[other, :, at], g_ss.at[2 + kind], g_rs.at[2 + kind], at_head(sibling))
-
     def x_copy(block, c):
         return remote(
             inner_hbm.at[:, part(other, c)],
@@ -414,7 +410,6 @@
         return jnp.where(left, cols[:, a : a + 1], cols[:, b : b + 1])
 
     group_copy(other, 0).wait_recv()
-    group_share(0).start()
 
     def send_far(s, _):
         pl.semaphore_wait(ready.at[me + 2 * s], 1)
@@ -426,7 +421,6 @@
     other_keeps = keeps_of(conv_flags(other, jnp.full((8, tokens), -1.0, F32)), tokens)
     pad_g[other, 0:RIM, :] = jnp.zeros((RIM, wide), F32)
     pad_x[other, 0:RIM, :] = jnp.zeros((RIM, half), F32)
-    group_share(0).wait_recv()
     pad_g[other, RIM:, 0:STATE_SIZE] = g_in[other, :, 0:STATE_SIZE].astype(F32)
     conv_groups(other, 0, other_keeps, tokens)
 
@@ -490,8 +484,8 @@
                 e_send[i] = state[r * depth : (r + 1) * depth, lanes].astype(BF16)
                 e_hop(i, upper).start()
 
+    lax.fori_loop(1, pair + 1, pass_on, 0)
     group_copy(other, 1).wait_recv()
-    group_share(1).start()
     pad_g[side, 0:RIM, STATE_SIZE:] = jnp.zeros((RIM, STATE_SIZE), F32)
     conv_groups(side, 1, own_keeps, tokens)
     pad_g[side, 0:RIM, STATE_SIZE:] = rim_g[side, :, STATE_SIZE:].astype(F32)
@@ -501,7 +495,6 @@
     crossing_pair = jnp.where(last_seg == prev_last, jnp.exp(total), 0.0)
     through = jnp.sum(jnp.where(spread, crossing_pair, 0.0), axis=0, keepdims=True)
     joined = cols[:, 24:25] == prev_last[0:1]
-    group_share(1).wait_recv()
     pad_g[other, RIM:, STATE_SIZE:] = g_in[other, :, STATE_SIZE:].astype(F32)
     conv_groups(other, 1, other_keeps, tokens)
     for b in range(2):
@@ -510,8 +503,6 @@
 
     for w in weights:
         w.start()
-
-    lax.fori_loop(1, pair + 1, pass_on, 0)
 
     for w in loads[10:]:
         w.wait()
@@ -665,7 +656,6 @@
         f_hop(c).wait_send()
     for kind in range(2):
         group_copy(side, kind).wait_send()
-        group_share(kind).wait_send()
     seg_copy(0, partner, 1 + side).wait_send()
 
     @pl.when(me < n_seq - 1)
@@ -755,8 +745,8 @@
         dma((2,)),
         dma((chunks,)),
         dma((chunks,)),
-        dma((4,)),
-        dma((4,)),
+        dma((2,)),
+        dma((2,)),
         dma((2,)),
         dma((2, 2)),
         dma((2, 2)),

time: 31.4 us -> 30.9 us (0.984)
  Pallas kernels: 29.7 us -> 29.2 us
    pallas_call x1, Pallas kernels: 29.7 us -> 29.2 us  [shards(): pl.pallas_call(functools.partial(kernel, n_seq, n_head), out_shape=jax.Sh...]
where the time goes in v4:
time: 30.9 us; the launch traced here: 30.7 us
  Pallas kernels  29.2 us (94%)
  local copies, waits for them, and re-layouts  1.57 us (5%)
    pallas_call x1, Pallas kernels, shards(): pl.pallas_call(functools.partial(kernel, n_seq, n_head), out_shape=jax.Sh...  29.2 us
    unnamed x1, local copies, waits for them, and re-layouts  1.57 us

profile of v4, /device:TPU:25, one launch (start us, length us, event | category | flops | bytes accessed | tf_op | source)
XLA Modules:
  0.0 30.7 jit_solution(17250821615490670386)
XLA Ops:
  0.0 29.2 %mixer.1 = bf16[128,512]{1,0:T(8,128)(2,1)} custom-call(bf16[128,768]{1,0:T(8,128)(2,1)} %inner_hbm.1, bf16[128,512]{1,0:T(8,128)(2,1)} %groups_hbm.1, bf16[128,768]{1,0:T(8,128)(2,1)} %gate_hbm.1, f32[12,128]{1,0:T(8,128)} %step_hbm.1, f32[12]{0:T(128)} %bias_hbm.1, f32[12]{0:T(128)} %decay_hbm.1, f32[4,768]{1,0:T(4,128)} %taps_inner_hbm.1, ...), custom_call_target="tpu_custom_call" | custom-call | tf_op jit(solution)/shard_map/mixer/pallas_call | solution.py:761
  29.2 1.6 %copy.17 = bf16[128,512]{1,0:T(8,128)(2,1)} copy(bf16[128,512]{1,0:T(8,128)(2,1)} %mixer.1) | data formatting | bytes 262144

commit v5 on v4

--- a/solution.py
+++ b/solution.py
@@ -16,6 +16,7 @@
 LANES = 128
 RIM = 16
 PIECES = 4
+CUTS = 4
 F32 = jnp.float32
 BF16 = jnp.bfloat16
 MESH = pl.DeviceIdType.MESH
@@ -622,32 +623,32 @@
     width = out_ref.shape[1]
 
     def product(j, part_of):
-        at = pl.ds(pl.multiple_of(j * width + part_of * (width // 2), LANES), width // 2)
+        at = pl.ds(pl.multiple_of(j * width + part_of * (width // CUTS), LANES), width // CUTS)
         return dot(both[:, :channels], mproj[:, at], (1, 0)) + dot(both[:, channels:], aproj[:, at], (1, 0))
 
     def rs_copy(i, target):
         return remote(rs_send.at[i], rs_recv.at[i], rs_ss.at[i], rs_rs.at[i], at_head(target))
 
-    to_pair = [rs_copy(h, sibling) for h in range(2)]
-    to_sibling = [rs_copy(2 + h, sibling) for h in range(2)]
-    to_opposite = [rs_copy(4 + h, opposite) for h in range(2)]
-    for h in range(2):
+    to_pair = [rs_copy(h, sibling) for h in range(CUTS)]
+    to_sibling = [rs_copy(CUTS + h, sibling) for h in range(CUTS)]
+    to_opposite = [rs_copy(2 * CUTS + h, opposite) for h in range(CUTS)]
+    for h in range(CUTS):
         rs_send[h] = product(opposite_sibling, h).astype(BF16)
         to_pair[h].start()
-    for h in range(2):
+    for h in range(CUTS):
         away = product(opposite, h)
         to_pair[h].wait_recv()
-        rs_send[4 + h] = (away + rs_recv[h].astype(F32)).astype(BF16)
+        rs_send[2 * CUTS + h] = (away + rs_recv[h].astype(F32)).astype(BF16)
         to_opposite[h].start()
-    for h in range(2):
-        rs_send[2 + h] = product(sibling, h).astype(BF16)
+    for h in range(CUTS):
+        rs_send[CUTS + h] = product(sibling, h).astype(BF16)
         to_sibling[h].start()
-    for h in range(2):
+    for h in range(CUTS):
         result = product(mine, h)
         to_sibling[h].wait_recv()
-        result = result + rs_recv[2 + h].astype(F32)
+        result = result + rs_recv[CUTS + h].astype(F32)
         to_opposite[h].wait_recv()
-        out_ref[:, h * (width // 2) : (h + 1) * (width // 2)] = (result + rs_recv[4 + h].astype(F32)).astype(BF16)
+        out_ref[:, h * (width // CUTS) : (h + 1) * (width // CUTS)] = (result + rs_recv[2 * CUTS + h].astype(F32)).astype(BF16)
 
     for copy in (*to_pair, *to_sibling, *to_opposite, step_copy(side)):
         copy.wait_send()
@@ -736,8 +737,8 @@
         pltpu.VMEM((tokens, channels + query.shape[1]), BF16),
         pltpu.VMEM(mproj.shape, BF16),
         pltpu.VMEM(aproj.shape, BF16),
-        pltpu.VMEM((6, tokens, out_width // 2), BF16),
-        pltpu.VMEM((6, tokens, out_width // 2), BF16),
+        pltpu.VMEM((3 * CUTS, tokens, out_width // CUTS), BF16),
+        pltpu.VMEM((3 * CUTS, tokens, out_width // CUTS), BF16),
         pltpu.VMEM((n_seq, query.shape[1] // HD * tokens, tokens), F32),
         *[pltpu.VMEM((query.shape[1] // HD * tokens, n), F32) for n in (tokens, tokens, HD)],
         pltpu.SemaphoreType.REGULAR((n_seq,)),
@@ -755,8 +756,8 @@
         *[dma((n_seq,)) for _ in range(5)],
         *[dma((PIECES * chunks,)) for _ in range(2)],
         *[dma((chunks,)) for _ in range(2)],
-        dma((6,)),
-        dma((6,)),
+        dma((3 * CUTS,)),
+        dma((3 * CUTS,)),
     ]
     return pl.pallas_call(
         functools.partial(kernel, n_seq, n_head),

time: 30.9 us -> 30.7 us (level)
  Pallas kernels: 29.2 us -> 28.8 us
    pallas_call x1, Pallas kernels: 29.2 us -> 28.8 us  [shards(): pl.pallas_call(functools.partial(kernel, n_seq, n_head), out_shape=jax.Sh...]
where the time goes in v5:
time: 30.7 us; the launch traced here: 30.4 us
  Pallas kernels  28.8 us (94%)
  local copies, waits for them, and re-layouts  1.57 us (5%)
    pallas_call x1, Pallas kernels, shards(): pl.pallas_call(functools.partial(kernel, n_seq, n_head), out_shape=jax.Sh...  28.8 us
    unnamed x1, local copies, waits for them, and re-layouts  1.57 us

profile of v5, /device:TPU:25, one launch (start us, length us, event | category | flops | bytes accessed | tf_op | source)
XLA Modules:
  0.0 30.4 jit_solution(5156356871777927247)
XLA Ops:
  0.0 28.8 %mixer.1 = bf16[128,512]{1,0:T(8,128)(2,1)} custom-call(bf16[128,768]{1,0:T(8,128)(2,1)} %inner_hbm.1, bf16[128,512]{1,0:T(8,128)(2,1)} %groups_hbm.1, bf16[128,768]{1,0:T(8,128)(2,1)} %gate_hbm.1, f32[12,128]{1,0:T(8,128)} %step_hbm.1, f32[12]{0:T(128)} %bias_hbm.1, f32[12]{0:T(128)} %decay_hbm.1, f32[4,768]{1,0:T(4,128)} %taps_inner_hbm.1, ...), custom_call_target="tpu_custom_call" | custom-call | tf_op jit(solution)/shard_map/mixer/pallas_call | solution.py:762
  28.8 1.6 %copy.17 = bf16[128,512]{1,0:T(8,128)(2,1)} copy(bf16[128,512]{1,0:T(8,128)(2,1)} %mixer.1) | data formatting | bytes 262144
